TPU v7x, 128 devices: a whole 4x4x4 slice. The times are simulated.
128 devices in a mesh: ctx: 16 (over x, y), tp: 8 (over z, core).
Axes of the slice: x: 4, y: 4, z: 4, core: 2. Of those that a mesh axis runs over, the one named last changes fastest.
Arguments:
- queries: bfloat16 [4096, 8192], P('ctx', 'tp'), may hold values from -16 to 16
- keys: bfloat16 [4096, 1024], P('ctx', 'tp'), may hold values from -4 to 4
- values: bfloat16 [4096, 1024], P('ctx', 'tp'), may hold values from -6 to 6
- out_weight: bfloat16 [8192, 8192], P('tp'), may hold values from -0.09375 to 0.09375
- ssm_input: bfloat16 [4096, 16384], P('ctx', 'tp'), may hold values from -6 to 6
- ssm_gate: bfloat16 [4096, 16384], P('ctx', 'tp'), may hold values from -6 to 6
- in_map: bfloat16 [4096, 1024], P('ctx', 'tp'), may hold values from -0.1796875 to 0.1796875
- out_map: bfloat16 [4096, 1024], P('ctx', 'tp'), may hold values from -1.796875 to 1.796875
- log_decay: float32 [4096, 256], P('ctx', 'tp'), may hold values from -1 to 0
- skip: float32 [256], P('tp'), may hold values from 0.5 to 1.5
- norm_gain: float32 [16384], P('tp'), may hold values from 0.1 to 1.9
Outputs:
- mixed: bfloat16 [4096, 8192], P('ctx', 'tp')
- ssm_out: bfloat16 [4096, 16384], P('ctx', 'tp')
All inputs are finite; a program needn't handle non-finite values.
Results may differ from a plain program's by a relative error of at most 0.019.
Values may be sent and summed in bfloat16 or wider, within the bound.
A program may use at most 128 MiB of HBM per device.

v0:
```python
import math

import jax
import jax.numpy as jnp
from jax import lax
from jax.sharding import PartitionSpec as P

HD = 128
HP = 64
NS = 128
BL = 128


def entering_2(shard, axis, combine, identity):
    length, position = (lax.axis_size(axis), lax.axis_index(axis))
    everything = jax.tree.map(
        lambda part, kind: lax.all_gather(part.astype(kind), axis),
        shard,
        (jnp.bfloat16, jnp.bfloat16),
    )
    start = jax.tree.map(
        lambda part, zero: jnp.broadcast_to(jnp.asarray(zero, part.dtype), part.shape),
        shard,
        identity,
    )

    def step(k, before):
        reached = k < position
        new = combine(
            before, jax.tree.map(lambda part, own: part[k].astype(own.dtype), everything, shard)
        )
        return jax.tree.map(lambda a, b: jnp.where(reached, a, b), new, before)

    return lax.fori_loop(0, length, step, start)


def score_block(running, query_part, query_positions, key_part, value_part, key_places):
    top_old, total_old, accum_old = running
    score_scale = 1.0 / math.sqrt(HD)
    scores = (
        jnp.einsum("krd,skd->krs", query_part, key_part, preferred_element_type=jnp.float32)
        * score_scale
    )
    visible = key_places[None, None, :] <= query_positions[None, :, None]
    scores = jnp.where(visible, scores, -jnp.inf)
    top_new = jnp.maximum(top_old, jnp.max(scores, axis=-1))
    shrink = jnp.exp(top_old - top_new)
    weights = jnp.exp(scores - top_new[..., None])
    total_new = total_old * shrink + jnp.sum(weights, axis=-1)
    accum_new = accum_old * shrink[..., None] + jnp.einsum(
        "krs,skd->krd", weights.astype(jnp.bfloat16), value_part, preferred_element_type=jnp.float32
    )
    return (top_new, total_new, accum_new)


def unchanged(running):
    return running


def ssm_mixer(ssm_input, ssm_gate, in_map, out_map, log_decay, skip, norm_gain):
    tok_rows = ssm_input.shape[0]
    local_heads = log_decay.shape[1]
    local_groups = in_map.shape[1] // NS
    group_heads = local_heads // local_groups
    block_count = tok_rows // BL
    inputs = ssm_input.reshape(block_count, BL, local_groups, group_heads, HP)
    input_maps = in_map.reshape(block_count, BL, local_groups, NS)
    output_maps = out_map.reshape(block_count, BL, local_groups, NS)
    decays = log_decay.reshape(block_count, BL, local_groups, group_heads)
    within = jnp.cumsum(decays, axis=1)
    pair_maps = jnp.einsum(
        "bign,bjgn->bgij", output_maps, input_maps, preferred_element_type=jnp.float32
    )
    ordered = within.transpose(0, 2, 3, 1)
    causal = lax.iota(jnp.int32, BL)[:, None] >= lax.iota(jnp.int32, BL)[None, :]
    gap_logs = jnp.where(causal, ordered[..., :, None] - ordered[..., None, :], 0.0)
    mixing = jnp.where(causal, pair_maps[:, :, None] * jnp.exp(gap_logs), 0.0).astype(jnp.bfloat16)
    inner_part = jnp.einsum(
        "bgkij,bjgkp->bigkp", mixing, inputs, preferred_element_type=jnp.float32
    )
    remaining = jnp.exp(within[:, -1:] - within)
    carried = (inputs.astype(jnp.float32) * remaining[..., None]).astype(jnp.bfloat16)
    block_states = jnp.einsum(
        "bjgkp,bjgn->bgkpn", carried, input_maps, preferred_element_type=jnp.float32
    )
    block_totals = within[:, -1]

    def advance(carry_state, block_item):
        total_decay, added_state = block_item
        return (jnp.exp(total_decay)[..., None, None] * carry_state + added_state, carry_state)

    zero_state = jnp.zeros((local_groups, group_heads, HP, NS), jnp.float32)
    end_state, before = lax.scan(advance, zero_state, (block_totals, block_states))
    maps_wide = output_maps.astype(jnp.float32)
    carried_out = jnp.einsum(
        "bign,bgkpn->bigkp", maps_wide, before, precision=lax.Precision.HIGHEST
    )
    skip_heads = skip.reshape(local_groups, group_heads)
    ssm_y = (
        inner_part
        + jnp.exp(within)[..., None] * carried_out
        + skip_heads[:, :, None] * inputs.astype(jnp.float32)
    )
    offsets = jnp.cumsum(block_totals, axis=0) - block_totals
    device_cum = within + offsets[:, None]
    device_decay = jnp.exp(jnp.sum(block_totals, axis=0))

    def combine(earlier, later):
        decay_early, state_early = earlier
        decay_late, state_late = later
        return (decay_early * decay_late, decay_late[..., None, None] * state_early + state_late)

    identity = (jnp.ones_like(device_decay), jnp.zeros_like(end_state))
    _, incoming = entering_2((device_decay, end_state), "ctx", combine, identity)
    entering = jnp.einsum("bign,gkpn->bigkp", maps_wide, incoming, precision=lax.Precision.HIGHEST)
    ssm_y = ssm_y + jnp.exp(device_cum)[..., None] * entering
    ssm_y = ssm_y.reshape(tok_rows, local_groups, group_heads * HP)
    gate_wide = ssm_gate.astype(jnp.float32).reshape(tok_rows, local_groups, group_heads * HP)
    gated = ssm_y * jax.nn.silu(gate_wide)
    normed = gated * lax.rsqrt(jnp.mean(gated * gated, axis=-1, keepdims=True) + 1e-05)
    normed = normed * norm_gain.reshape(local_groups, group_heads * HP)
    return normed.reshape(tok_rows, local_heads * HP).astype(jnp.bfloat16)


def local(
    queries,
    keys,
    values,
    out_weight,
    ssm_input,
    ssm_gate,
    in_map,
    out_map,
    log_decay,
    skip,
    norm_gain,
):
    tok_rows = queries.shape[0]
    half_rows = tok_rows // 2
    kv_heads = keys.shape[1] // HD
    query_heads = queries.shape[1] // HD
    per_head = query_heads // kv_heads
    cycle_place = lax.axis_index("ctx")
    local_rows = lax.iota(jnp.int32, tok_rows)
    query_cols = queries.shape[1]
    query_pos = cycle_place * tok_rows + local_rows
    group_queries = []
    group_pos = []
    for query_half in range(2):
        rows_part = queries[query_half * half_rows : (query_half + 1) * half_rows]
        rows_part = rows_part.reshape(half_rows, kv_heads, per_head, HD).transpose(1, 0, 2, 3)
        group_queries.append(rows_part.reshape(kv_heads, half_rows * per_head, HD))
        group_pos.append(
            jnp.repeat(query_pos[query_half * half_rows : (query_half + 1) * half_rows], per_head)
        )
    group_rows = half_rows * per_head
    start_state = (
        jnp.full((kv_heads, group_rows), -1e30, jnp.float32),
        jnp.zeros((kv_heads, group_rows), jnp.float32),
        jnp.zeros((kv_heads, group_rows, HD), jnp.float32),
    )
    running = (start_state, start_state)
    key_rows = lax.all_gather(keys, "ctx", axis=0, tiled=True)
    value_rows = lax.all_gather(values, "ctx", axis=0, tiled=True)
    row_count = key_rows.shape[0]
    key_pos = lax.iota(jnp.int32, row_count)
    key_heads = key_rows.reshape(row_count, kv_heads, HD)
    value_heads = value_rows.reshape(row_count, kv_heads, HD)
    step_rows = 512
    updated = []
    for visit_query_half in range(2):
        query_part = group_queries[visit_query_half]
        query_positions = group_pos[visit_query_half]

        def absorb(state_now):

            def inner_step(block_number, state_inner):
                low_row = block_number * step_rows
                return score_block(
                    state_inner,
                    query_part,
                    query_positions,
                    lax.dynamic_slice_in_dim(key_heads, low_row, step_rows, 0),
                    lax.dynamic_slice_in_dim(value_heads, low_row, step_rows, 0),
                    lax.dynamic_slice_in_dim(key_pos, low_row, step_rows, 0),
                )

            return lax.fori_loop(0, row_count // step_rows, inner_step, state_now)

        skipped = jnp.min(key_pos) > jnp.max(query_positions)
        updated.append(lax.cond(skipped, unchanged, absorb, running[visit_query_half]))
    final_states = tuple(updated)
    halves_out = []
    for query_half in range(2):
        top_final, total_final, accum_final = final_states[query_half]
        normalized = accum_final / total_final[..., None]
        normalized = normalized.reshape(kv_heads, half_rows, per_head, HD).transpose(1, 0, 2, 3)
        halves_out.append(normalized.reshape(half_rows, query_cols).astype(jnp.bfloat16))
    attention = jnp.concatenate(halves_out, axis=0)
    summed = lax.psum_scatter(
        lax.dot_general(
            out_weight, attention, (((0,), (1,)), ((), ())), preferred_element_type=jnp.float32
        ).astype(jnp.bfloat16),
        "tp",
        scatter_dimension=0,
        tiled=True,
    ).astype(jnp.float32)
    mixed = summed.T.astype(jnp.bfloat16)
    ssm_out = ssm_mixer(ssm_input, ssm_gate, in_map, out_map, log_decay, skip, norm_gain)
    return (mixed, ssm_out)


def solution(mesh):
    in_specs = (
        P("ctx", "tp"),
        P("ctx", "tp"),
        P("ctx", "tp"),
        P("tp", None),
        P("ctx", "tp"),
        P("ctx", "tp"),
        P("ctx", "tp"),
        P("ctx", "tp"),
        P("ctx", "tp"),
        P("tp"),
        P("tp"),
    )
    out_specs = (P("ctx", "tp"), P("ctx", "tp"))
    return jax.shard_map(local, mesh=mesh, in_specs=in_specs, out_specs=out_specs, check_vma=False)
```

profile of v0, /device:TPU:0, one launch (start us, length us, event | category | flops | bytes accessed | tf_op | source)
XLA Modules:
  0.0 273.4 jit_solution(4269620219326701846)
XLA Ops:
  11.2 1.5 copy.45
  13.0 1.8 multiply_convert_fusion.1
  15.2 2.6 while.65
  22.3 2.4 fusion.42
  24.7 30.6 %all-gather.6.cloned.1.call-done = bf16[4096,128]{1,0:T(8,128)(2,1)} async-done(((bf16[256,128]{1,0:T(8,128)(2,1)}), bf16[4096,128]{1,0:T(8,128)(2,1)}) %all-gather.6.cloned.1.call-update) | async-done | bytes 1048592 | tf_op jit(solution)/shard_map/all_gather | solution.py:163
  55.3 44.0 %all-gather.8.cloned.1.call-done = bf16[4096,128]{1,0:T(8,128)(2,1)} async-done(((bf16[256,128]{1,0:T(8,128)(2,1)}), bf16[4096,128]{1,0:T(8,128)(2,1)}) %all-gather.8.cloned.1.call-update) | async-done | bytes 1048592 | tf_op jit(solution)/shard_map/all_gather | solution.py:164
  99.4 29.2 %conditional.2 = (f32[1,1024]{1,0:T(1,128)S(1)}, f32[1,1024,128]{2,1,0:T(8,128)S(1)}) conditional(s32[]{:T(128)} %convert_element_type.135, (bf16[256,1024]{1,0:T(8,128)(2,1)}, s32[4096]{0:T(1024)S(1)}, s32[128,8]{1,0:T(8,128)S(1)}, bf16[4096,1,128]{2,0,1:T(8,128)(2,1)}, bf16[4096,1,128]{2,0,1:T(8,128)(2,1)}) %tuple.191, () %tuple.71), branch_computations={%region_1.6_spmd, %region_6.0_spmd} | conditional | flops 273028096 | bytes 9013615 | solution.py:191
  100.6 27.9 %while.63 = (s32[]{:T(128)}, f32[1,1024]{1,0:T(1,128)S(1)}, f32[1,1024]{1,0:T(1,128)S(1)}, f32[1,1024,128]{2,1,0:T(8,128)S(1)}, s32[4096]{0:T(1024)S(1)}, /*inde...) while((s32[]{:T(128)}, f32[1,1024]{1,0:T(1,128)S(1)}, ...), condition=%wide.wide.region_5.0_spmd.clone, body=%wide.wide.region_2.4_spmd.clone.sunk | while | flops 273028096 | bytes 7940299 | solution.py:188
  100.7 1.4 fusion.112
  102.4 1.6 fusion.116
  104.2 1.4 fusion.112
  105.9 1.6 fusion.116
  107.7 1.4 fusion.112
  109.4 1.6 fusion.116
  111.2 1.4 fusion.112
  112.9 1.6 fusion.116
  114.7 1.4 fusion.112
  116.4 1.6 fusion.116
  118.2 1.4 fusion.112
  119.9 1.6 fusion.116
  121.6 1.4 fusion.112
  123.4 1.6 fusion.116
  125.1 1.4 fusion.112
  126.9 1.6 fusion.116
  129.0 30.9 %conditional.3 = (f32[1,1024]{1,0:T(1,128)S(1)}, f32[1,1024,128]{2,1,0:T(8,128)S(1)}) conditional(s32[]{:T(128)} %convert_element_type.138, (bf16[256,1024]{1,0:T(8,128)(2,1)}, s32[4096]{0:T(1024)S(1)}, s32[128,8]{1,0:T(8,128)S(1)}, bf16[4096,1,128]{2,0,1:T(8,128)(2,1)}, bf16[4096,1,128]{2,0,1:T(8,128)(2,1)}) %tuple.192, () %tuple.73), branch_computations={%region_8.13_spmd, %region_13.14_spmd} | conditional | flops 273028096 | bytes 9013615 | solution.py:191
  130.9 28.9 %while.64 = (s32[]{:T(128)}, f32[1,1024]{1,0:T(1,128)S(1)}, f32[1,1024]{1,0:T(1,128)S(1)}, f32[1,1024,128]{2,1,0:T(8,128)S(1)}, s32[4096]{0:T(1024)S(1)}, /*inde...) while((s32[]{:T(128)}, f32[1,1024]{1,0:T(1,128)S(1)}, ...), condition=%wide.wide.region_12.0_spmd.clone, body=%wide.wide.region_9.0_spmd.clone.sunk | while | flops 273028096 | bytes 7940299 | solution.py:188
  131.0 1.5 fusion.105
  132.8 1.6 fusion.109
  134.6 1.5 fusion.105
  136.5 1.6 fusion.109
  138.2 1.5 fusion.105
  140.1 1.6 fusion.109
  141.8 1.5 fusion.105
  143.7 1.6 fusion.109
  145.5 1.5 fusion.105
  147.3 1.6 fusion.109
  149.1 1.5 fusion.105
  150.9 1.6 fusion.109
  152.7 1.5 fusion.105
  154.6 1.6 fusion.109
  156.3 1.5 fusion.105
  158.2 1.6 fusion.109
  160.2 12.3 %fusion.33 = bf16[8192,256]{0,1:T(8,128)(2,1)} fusion(bf16[1024,8192]{1,0:T(8,128)(2,1)} %param.26, bf16[128,1024]{1,0:T(8,128)(2,1)S(1)} %convert_element_type.140, bf16[128,1024]{1,0:T(8,128)(2,1)S(1)} %convert_element_type.137), kind=kOutput, calls=%fused_computation.51 | convolution fusion | flops 4298113024 | bytes 21495808 | tf_op jit(solution)/shard_map/dot_general | solution.py:201
  173.7 3.2 %reshape.364 = f32[2,128,1,32,64]{4,3,1,0,2:T(8,128)} reshape(bf16[256,2048]{1,0:T(8,128)(2,1)S(1)} %copy-done.1) | data formatting | bytes 3145728 | tf_op jit(solution)/shard_map/convert_element_type | solution.py:82
  178.4 38.3 %all-reduce = bf16[512]{0:T(512)(128)(2,1)S(1)} all-reduce(bf16[512]{0:T(512)(128)(2,1)S(1)} %dynamic-update-slice), channel_id=2, replica_groups=mesh['ctx'=16,'tp'=8] {'ctx'}, use_global_device_ids=true, to_apply=%add | all-reduce | flops 512 | bytes 2048
  217.5 4.8 %copy.53 = f32[2,128,1,32,64]{1,4,3,0,2:T(8,128)} copy(f32[2,128,1,32,64]{4,3,1,0,2:T(8,128)} %reshape.364) | data formatting | bytes 4194304 | tf_op jit(solution)/shard_map/convert_element_type | solution.py:82
  222.3 1.6 copy.59
  223.9 3.3 %fusion.34 = f32[2,32,128,64]{2,3,1,0:T(8,128)} fusion(f32[2,32,128]{2,1,0:T(8,128)S(1)} %copy.43, f32[2,128,128]{2,1,0:T(8,128)S(1)} %copy-done.9, pred[128,128]{1,0:T(8,128)(4,1)S(1)} %iota_compare_fusion, bf16[2,128,32,64]{1,0,3,2:T(2,128)(2,1)S(1)} %copy-done.3), kind=kOutput, calls=%fused_computation.55 | convolution fusion | flops 139460608 | bytes 3325952 | tf_op jit(solution)/shard_map/bgkij,bjgkp->bigkp/dot_general | solution.py:78
  227.2 31.1 %while.66 = (s32[]{:T(128)}, f32[1,32,64,128]{3,2,1,0:T(8,128)S(1)}, s32[]{:T(128)}, bf16[16,1,32]{2,1,0:T(2,128)(2,1)}, bf16[16,1,32,64,128]{4,3,2,1,0:T(8,128)(2,1)}, /*index=5*/s32[]{:T(128)}, s32[]{:T(128)}) while((s32[]{:T(128)}, f32[1,32,64,128]{3,2,1,0:T(8,128)S(1)}, s32[]{:T(128)}, bf16[16,1,32]{2,1,0:T(2,128)(2,1)}, ...), condition=%wide.region_21.22_spmd.clone, body=%wide.region_20.21_spmd.clone.sunk | while | flops 1310756 | bytes 2621865 | solution.py:34
  227.8 1.3 fusion.102
  229.8 1.3 fusion.102
  231.7 1.3 fusion.102
  233.6 1.3 fusion.102
  235.6 1.3 fusion.102
  237.5 1.3 fusion.102
  239.4 1.3 fusion.102
  241.4 1.3 fusion.102
  243.4 1.3 fusion.102
  247.2 1.3 fusion.102
  249.2 1.3 fusion.102
  251.1 1.3 fusion.102
  258.3 3.9 %fusion.39 = f32[2,128,1,32,64]{1,4,3,0,2:T(8,128)S(1)} fusion(f32[2,32,64,128]{3,2,1,0:T(8,128)} %fusion.42, f32[2,32,128,64]{2,3,1,0:T(8,128)} %fusion.34, f32[2,128,1,32,64]{1,4,3,0,2:T(8,128)} %copy.53, bf16[2,128,128,1]{2,1,3,0:T(8,128)(2,1)S(1)} %bitcast.201, f32[1,32,64,128]{3,2,1,0:T(8,128)S(1)} %get-tuple-element.478, f32[2,128,32]{1,2,0:T(8,128)S(1)} %copy.54, ...), kind=kOutput, calls=%fused_computation.61 | convolution fusion | flops 808452096 | bytes 9568384 | tf_op jit(solution)/shard_map/bign,gkpn->bigkp/dot_general | solution.py:115
  262.2 1.7 copy.58
  265.4 1.4 copy.60
  (192 shorter events, 40.9 us)
Async XLA Ops:
  7.2 14.3 %copy-start = (bf16[256,128]{1,0:T(8,128)(2,1)S(1)}, bf16[256,128]{1,0:T(8,128)(2,1)}, u32[]{:S(2)}) copy-start(bf16[256,128]{1,0:T(8,128)(2,1)} %param.30) | copy-start | bytes 196612
  7.2 48.1 %all-gather.6.cloned.1.call-start = ((), (), s32[]{:S(2)}) async-start(), calls=%async_computation.1 | async-start | bytes 1114112 | tf_op jit(solution)/shard_map/all_gather | solution.py:163
  7.9 91.4 %all-gather.8.cloned.1.call-start = ((), (), s32[]{:S(2)}) async-start(), calls=%async_computation.2 | async-start | bytes 1114112 | tf_op jit(solution)/shard_map/all_gather | solution.py:164
  8.7 218.5 %all-gather.10.cloned.1.call-start = ((), (), s32[]{:S(2)}) async-start(), calls=%async_computation.4 | async-start | bytes 8912896 | tf_op jit(solution)/shard_map/all_gather | solution.py:17
  12.6 2.2 copy-start.6
  12.9 1.9 copy-start.2
  17.9 4.4 %copy-start.4 = (f32[2,1,32,64,128]{4,3,2,1,0:T(8,128)S(1)}, f32[2,1,32,64,128]{4,3,2,1,0:T(8,128)}, u32[]{:S(2)}) copy-start(f32[2,1,32,64,128]{4,3,2,1,0:T(8,128)} %get-tuple-element.476) | copy-start | bytes 6291460
  18.8 248.1 %reduce-scatter.2.cloned.1.call-start = ((), (), s32[]{:S(2)}) async-start(), calls=%async_computation.3 | async-start | bytes 4718592 | tf_op jit(solution)/shard_map/reduce_scatter | solution.py:200
  99.4 1.2 copy-start.8
  129.0 1.9 copy-start.7
  172.4 1.2 copy-start.1
  173.7 3.2 %copy-start.12 = (u32[128]{0:T(128)S(1)}, u32[128]{0:T(128)}, u32[]{:S(2)}) copy-start(u32[128]{0:T(128)} %constant.179) | copy-start | bytes 1540
  173.7 4.4 %copy-start.13 = (bf16[32]{0:T(256)(128)(2,1)S(1)}, bf16[32]{0:T(256)(128)(2,1)}, u32[]{:S(2)}) copy-start(bf16[32]{0:T(256)(128)(2,1)} %exponential_convert_fusion) | copy-start | bytes 196
  173.7 43.7 %copy-start.5 = (f32[2,128,32]{2,1,0:T(8,128)S(1)}, f32[2,128,32]{2,1,0:T(8,128)}, u32[]{:S(2)}) copy-start(f32[2,128,32]{2,1,0:T(8,128)} %get-tuple-element.668) | copy-start | bytes 98308
  222.3 1.6 copy-start.3
  222.3 1.6 copy-start.9
  227.2 31.1 %copy-start.11 = (f32[32]{0:T(128)S(1)}, f32[32]{0:T(128)}, u32[]{:S(2)}) copy-start(f32[32]{0:T(128)} %param.32) | copy-start | bytes 388
  263.9 0.8 copy-start.10
Sparse Core Ops, SparseCore 0:
  10.2 45.0 all-gather.5
  57.4 41.8 all-gather.7
  101.4 69.9 all-gather.9
  174.2 38.0 reduce-scatter.1
where the time goes:
time: 275 us; the launch traced here: 273 us
  waiting for transfers between devices  76 us (28%)
  matrix products  72 us (26%)
  other arithmetic  46 us (17%)
  blocking collectives  38.3 us (14%)
  local copies, waits for them, and re-layouts  23.6 us (9%)
  between operations  16 us (6%)
    all_gather x1, waiting for transfers between devices, local(): value_rows = lax.all_gather(values, 'ctx', axis=0, tiled=True)  44 us
    unnamed x1, blocking collectives  38.3 us
    all_gather x1, waiting for transfers between devices, local(): key_rows = lax.all_gather(keys, 'ctx', axis=0, tiled=True)  30.6 us
    dot_general x16, matrix products, score_block(): jnp.einsum('krs,skd->krd', weights.astype(jnp.bfloat16), value_part, pref...  26.1 us
    dot_general x16, matrix products, score_block(): jnp.einsum('krd,skd->krs', query_part, key_part, preferred_element_type=j...  22.8 us
    select_n x16, other arithmetic, step(): return jax.tree.map(lambda a, b: jnp.where(reached, a, b), new, before)  20.7 us
    dot_general x1, matrix products, local(): lax.dot_general(out_weight, attention, (((0,), (1,)), ((), ())), preferre...  12.3 us
    convert_element_type x16, other arithmetic, step(): part[k].astype(own.dtype)  10.1 us
  transfers between devices with their start and end apart: 4, of which 2 were waited for; matrix products, arithmetic and copies ran while one was open for 51% of the time, Pallas kernels for 0%

commit v1 on v0

v1 whole, which is shorter than its diff:
```python
import math

import jax
import jax.numpy as jnp
from jax import lax
from jax.experimental import pallas as pl
from jax.experimental.pallas import tpu as pltpu
from jax.sharding import PartitionSpec as P

HD = 128
HP = 64
NS = 128
BL = 128
SIDE = 4
RANKS = SIDE * SIDE
HEADS = 8
MIXERS = 32
TOK = 256
HALF = 128
WIDE = 1024
FEATURES = MIXERS * HP
PIECE = NS + 16
MESH = pl.DeviceIdType.MESH
F32 = jnp.float32
BF16 = jnp.bfloat16
SCORE_SCALE = math.log2(math.e) / math.sqrt(HD)


def dot(a, b):
    return lax.dot_general(a, b, (((1,), (0,)), ((), ())), preferred_element_type=F32)


def dot_t(a, b):
    return lax.dot_general(a, b, (((1,), (1,)), ((), ())), preferred_element_type=F32)


def iota(shape, dim):
    return lax.broadcasted_iota(jnp.int32, shape, dim)


def split3(v):
    hi = v.astype(BF16)
    rest = v - hi.astype(F32)
    mid = rest.astype(BF16)
    lo = (rest - mid.astype(F32)).astype(BF16)
    return hi, mid, lo


def lane_split(v):
    hi, mid, lo = split3(v)
    group = iota(v.shape, 1) // MIXERS
    parts = jnp.where(
        group == 0,
        hi.astype(F32),
        jnp.where(group == 1, mid.astype(F32), jnp.where(group == 2, lo.astype(F32), 0.0)),
    )
    return parts.astype(BF16)


def spread(first_head, lanes_per_head):
    return (
        iota((128, 256), 0) % MIXERS == first_head + iota((128, 256), 1) // lanes_per_head
    ).astype(F32).astype(BF16)


def kernel(
    q_hbm, k_hbm, v_hbm, w_hbm, x_hbm, g_hbm, b_hbm, c_hbm, ld_hbm, skip_hbm, gain_hbm,
    mixed_hbm, ssm_hbm,
    qv, kv, wv, xv, gv, bv, cv, ldv, skv, gnv,
    cumsplit, cum_rows, pair_maps, bt, remsplit, expsplit, expx, skx, inner, s0buf,
    st_send, st_recv, in_send, in_recv, ssm_v,
    acc, top, att, own, xs, xr, fs, fr, ns, nr, mixed_v,
    load_sem, kv_send, kv_recv, sts, str_, ins, inr, xss, xsr, fss, fsr, nss, nsr, out_sem,
):
    rank = lax.axis_index("ctx")
    tp = lax.axis_index("tp")
    x, y = rank // SIDE, rank % SIDE
    z, core = tp // 2, tp % 2
    up = 2 * ((z + 1) % SIDE) + core
    down = 2 * ((z + SIDE - 1) % SIDE) + core
    partner = 2 * z + 1 - core

    loads = [
        (k_hbm, kv.at[rank, 0]),
        (v_hbm, kv.at[rank, 1]),
        (ld_hbm, ldv),
        (skip_hbm, skv),
        (x_hbm, xv),
        (b_hbm, bv),
        (c_hbm, cv),
        (q_hbm, qv),
        (w_hbm, wv),
        (g_hbm, gv),
        (gain_hbm, gnv),
    ]
    copies = [pltpu.make_async_copy(a, b, load_sem.at[i]) for i, (a, b) in enumerate(loads)]
    for copy in copies:
        copy.start()

    barrier = pltpu.get_barrier_semaphore()

    def greet(d, _):
        pl.semaphore_signal(barrier, inc=1, device_id=((rank + d) % RANKS, tp), device_id_type=MESH)
        return 0

    lax.fori_loop(1, RANKS, greet, 0)
    for other in (partner, up, down):
        pl.semaphore_signal(barrier, inc=1, device_id=(rank, other), device_id_type=MESH)
    pl.semaphore_wait(barrier, RANKS - 1 + 3)

    def kv_copy(block, dest, sem):
        return pltpu.make_async_remote_copy(
            src_ref=kv.at[block],
            dst_ref=kv.at[block],
            send_sem=kv_send.at[sem],
            recv_sem=kv_recv.at[block],
            device_id=(dest, tp),
            device_id_type=MESH,
        )

    copies[0].wait()
    copies[1].wait()
    for d in range(1, SIDE):
        kv_copy(rank, SIDE * x + (y + d) % SIDE, d - 1).start()
    for xd in range(1, SIDE):

        @pl.when((core == 1) & (xd > x))
        def _():
            kv_copy(rank, SIDE * xd + y, 2 + xd).start()

    copies[2].wait()
    copies[3].wait()
    repeat = (iota((MIXERS, 128), 1) % MIXERS == iota((MIXERS, 128), 0)).astype(F32).astype(BF16)
    lower = (iota((BL, BL), 0) >= iota((BL, BL), 1)).astype(F32).astype(BF16)
    decays = [dot(part, repeat) for part in split3(ldv[...])]
    decays = (decays[0] + decays[1]) + decays[2]
    for b in range(2):
        rows = slice(b * BL, (b + 1) * BL)
        cum = [dot(lower, part) for part in split3(decays[rows])]
        cum = (cum[0] + cum[1]) + cum[2]
        cumsplit[rows, :] = lane_split(cum)
        cum_rows[b] = cum.T
        expsplit[rows, :] = lane_split(jnp.exp(cum))
        remsplit[rows, :] = lane_split(jnp.exp(cum[BL - 1 : BL] - cum))
    skips = [dot(part, repeat) for part in split3(jnp.broadcast_to(skv[...], (8, MIXERS)))]
    skip_split = lane_split((skips[0] + skips[1]) + skips[2])
    copies[4].wait()
    copies[5].wait()
    for b in range(2):
        bt[b] = bv[b * BL : (b + 1) * BL, :].astype(F32).T.astype(BF16)

    def state_chunk(ci, _):
        cols = pl.ds(pl.multiple_of(ci * 256, 256), 256)
        e = spread(4 * ci, HP)
        ex = dot(expsplit[...], e)
        expx[:, cols] = ex
        skx[:, cols] = dot(skip_split, e)
        carried = (xv[:, cols].astype(F32) * dot(remsplit[...], e)).astype(BF16)
        s0 = dot(bt[0], carried[:BL])
        s1 = dot(bt[1], carried[BL:])
        s0buf[:, cols] = s0
        d0, d1 = ex[BL - 1 : BL], ex[2 * BL - 1 :]
        end = (d1 * s0 + s1).astype(BF16)
        decay = d0 * d1
        hi = decay.astype(BF16).astype(F32)
        row = iota((16, 256), 0)
        tail = jnp.where(row == 0, hi, jnp.where(row == 1, decay - hi, 0.0)).astype(BF16)
        for u in range(2):
            st_send[2 * ci + u, :NS, :] = end[:, u * 128 : (u + 1) * 128]
            st_send[2 * ci + u, NS:, :] = tail[:, u * 128 : (u + 1) * 128]
        return 0

    lax.fori_loop(0, FEATURES // 256, state_chunk, 0)

    def state_copy(piece):
        return pltpu.make_async_remote_copy(
            src_ref=st_send.at[piece],
            dst_ref=st_recv.at[rank],
            send_sem=sts.at[piece],
            recv_sem=str_.at[rank],
            device_id=(piece, tp),
            device_id_type=MESH,
        )

    def send_state(d, _):
        state_copy((rank + d) % RANKS).start()
        return 0

    lax.fori_loop(1, RANKS, send_state, 0)
    st_recv[rank] = st_send[rank]

    for d in range(1, SIDE):
        kv_copy(SIDE * x + (y + d) % SIDE, rank, 0).wait_recv()
    for xd in range(1, SIDE):
        for yb in range(SIDE):

            @pl.when((core == 0) & (xd > x))
            def _():
                kv_copy(SIDE * x + yb, SIDE * xd + y, 3 + 4 * (xd - 1) + yb).start()

    for xb in range(SIDE - 1):

        @pl.when((core == 1) & (xb < x))
        def _():
            kv_copy(SIDE * xb + y, rank, 0).wait_recv()
            for d in range(1, SIDE):
                kv_copy(SIDE * xb + y, SIDE * x + (y + d) % SIDE, 6 + 3 * xb + d - 1).start()

    copies[6].wait()
    for b in range(2):
        rows = slice(b * BL, (b + 1) * BL)
        maps = dot_t(cv[rows, :], bv[rows, :])
        pair_maps[b] = jnp.where(iota((BL, BL), 0) >= iota((BL, BL), 1), maps, 0.0)
    low_lanes = (iota((BL, 128), 1) < HP).astype(F32).astype(BF16)
    high_lanes = (iota((BL, 128), 1) >= HP).astype(F32).astype(BF16)

    def inner_pair(p, _):
        cols = pl.ds(pl.multiple_of(p * 128, 128), 128)
        down_col = dot(cumsplit[...], spread(2 * p, 128))
        for b in range(2):
            rows = slice(b * BL, (b + 1) * BL)
            mixing = []
            for u in range(2):
                gap = down_col[rows, u * 128 : (u + 1) * 128] - cum_rows[b, pl.ds(2 * p + u, 1), :]
                mixing.append((pair_maps[b] * jnp.exp(jnp.minimum(gap, 0.0))).astype(BF16))
            xp = xv[rows, cols]
            both = jnp.concatenate([xp * low_lanes, xp * high_lanes], axis=0)
            inner[rows, cols] = dot(jnp.concatenate(mixing, axis=1), both)
        return 0

    lax.fori_loop(0, MIXERS // 2, inner_pair, 0)

    def in_copy(dest):
        return pltpu.make_async_remote_copy(
            src_ref=in_send.at[dest],
            dst_ref=in_recv.at[rank],
            send_sem=ins.at[dest],
            recv_sem=inr.at[rank],
            device_id=(dest, tp),
            device_id_type=MESH,
        )

    def prefix(i, before):
        @pl.when(i != rank)
        def _():
            pltpu.make_async_copy(st_recv.at[i], st_recv.at[i], str_.at[i]).wait()

        in_send[i] = before.astype(BF16)

        @pl.when(i != rank)
        def _():
            in_copy(i).start()

        tail = st_recv[i, NS:, :].astype(F32)
        return (tail[0:1] + tail[1:2]) * before + st_recv[i, :NS, :].astype(F32)

    lax.fori_loop(0, RANKS, prefix, jnp.zeros((NS, 128), F32))
    in_recv[rank] = in_send[rank]

    copies[7].wait()
    ones = jnp.ones((WIDE, HD), BF16)

    def absorb(half, row_index, first):
        def pair(hp, _):
            for u in range(2):
                h = 2 * hp + u
                q = qv[half * HALF : (half + 1) * HALF, pl.ds(pl.multiple_of(h * HD, HD), HD)]
                keys = kv[pl.ds(SIDE * row_index, SIDE), 0].reshape(WIDE, HD)
                values = kv[pl.ds(SIDE * row_index, SIDE), 1].reshape(WIDE, HD)
                values = jnp.concatenate([values, ones], axis=1)
                scores = dot_t(q, keys)
                if first:
                    place = iota((HALF, WIDE), 0) + (y * TOK + half * HALF)
                    scores = jnp.where(iota((HALF, WIDE), 1) <= place, scores, -1e30)
                    new = jnp.max(scores, axis=1, keepdims=True)
                else:
                    old = top[h, :, 0:1]
                    new = jnp.maximum(old, jnp.max(scores, axis=1, keepdims=True))
                weights = jnp.exp2(scores * SCORE_SCALE - new * SCORE_SCALE).astype(BF16)
                add = dot(weights, values)
                if first:
                    acc[h] = add
                else:
                    acc[h] = acc[h] * jnp.exp2((old - new) * SCORE_SCALE) + add
                top[h] = jnp.broadcast_to(new, (HALF, 128))
            return 0

        lax.fori_loop(0, HEADS // 2, pair, 0)

    def wait_row(row_index):
        for yb in range(SIDE):

            @pl.when((core == 0) | (yb != y))
            def _():
                kv_copy(SIDE * row_index + yb, rank, 0).wait_recv()

    def finish(half):
        def one(h, _):
            a = acc[h]
            att[:, pl.ds(pl.multiple_of(h * HD, HD), HD)] = (a[:, :HD] / a[:, HD:]).astype(BF16)
            return 0

        lax.fori_loop(0, HEADS, one, 0)

    def project(block):
        cols = pl.ds(pl.multiple_of(block * WIDE, WIDE), WIDE)
        return dot(att[...], wv[:, cols])

    def far_first(i):
        return (2 + i) % SIDE

    def xs_copy(half, d):
        return pltpu.make_async_remote_copy(
            src_ref=xs.at[half, d],
            dst_ref=xr.at[half, d],
            send_sem=xss.at[half, d],
            recv_sem=xsr.at[half, d],
            device_id=(rank, partner),
            device_id_type=MESH,
        )

    def ring_copy(src, dst, send, recv, half, way):
        return pltpu.make_async_remote_copy(
            src_ref=src.at[half, way],
            dst_ref=dst.at[half, way],
            send_sem=send.at[half, way],
            recv_sem=recv.at[half, way],
            device_id=(rank, up if way == 0 else down),
            device_id_type=MESH,
        )

    def far_copy(half, way):
        return ring_copy(fs, fr, fss, fsr, half, way)

    def near_copy(half, way):
        return ring_copy(ns, nr, nss, nsr, half, way)

    STEP = 32

    def project_and_send(half):
        def for_partner(i, _):
            d = far_first(i)
            xs[half, d] = project(2 * ((z + d) % SIDE) + 1 - core).astype(BF16)
            xs_copy(half, d).start()
            return 0

        def for_own(i, _):
            d = far_first(i)
            own[half, d] = project(2 * ((z + d) % SIDE) + core)
            return 0

        lax.fori_loop(0, SIDE, for_partner, 0)
        for_own(0, 0)
        xs_copy(half, 2).wait_recv()
        for way in range(2):

            def far_sum(t, _):
                rows = pl.ds(pl.multiple_of(64 * way + t * STEP, STEP), STEP)
                fs[half, way, pl.ds(pl.multiple_of(t * STEP, STEP), STEP), :] = (
                    own[half, 2, rows, :] + xr[half, 2, rows, :].astype(F32)
                ).astype(BF16)
                return 0

            lax.fori_loop(0, 64 // STEP, far_sum, 0)
            far_copy(half, way).start()
        lax.fori_loop(1, SIDE, for_own, 0)

    def near(half):
        for way in range(2):
            d = 1 if way == 0 else 3
            xs_copy(half, d).wait_recv()
            far_copy(half, way).wait_recv()

            def near_sum(t, _):
                for has_far in (True, False):
                    start = 64 * way if has_far else 64 - 64 * way
                    rows = pl.ds(pl.multiple_of(start + t * STEP, STEP), STEP)
                    total = own[half, d, rows, :] + xr[half, d, rows, :].astype(F32)
                    if has_far:
                        far = fr[half, way, pl.ds(pl.multiple_of(t * STEP, STEP), STEP), :]
                        total = total + far.astype(F32)
                    ns[half, way, rows, :] = total.astype(BF16)
                return 0

            lax.fori_loop(0, 64 // STEP, near_sum, 0)
            near_copy(half, way).start()

    def last(half):
        xs_copy(half, 0).wait_recv()
        near_copy(half, 0).wait_recv()
        near_copy(half, 1).wait_recv()

        def last_sum(t, _):
            rows = pl.ds(pl.multiple_of(t * STEP, STEP), STEP)
            total = own[half, 0, rows, :] + xr[half, 0, rows, :].astype(F32)
            total = total + nr[half, 0, rows, :].astype(F32) + nr[half, 1, rows, :].astype(F32)
            mixed_v[half, rows, :] = total.astype(BF16)
            return 0

        lax.fori_loop(0, HALF // STEP, last_sum, 0)
        mixed_out(half).start()

    def mixed_out(half):
        return pltpu.make_async_copy(
            mixed_v.at[half], mixed_hbm.at[half * HALF : (half + 1) * HALF], out_sem.at[half]
        )

    absorb(0, x, True)
    for i in range(1, SIDE):

        @pl.when(i <= x)
        def _():
            wait_row(x - i)
            absorb(0, x - i, False)

    finish(0)
    copies[8].wait()
    project_and_send(0)

    absorb(1, x, True)
    for i in range(1, SIDE):

        @pl.when(i <= x)
        def _():
            absorb(1, x - i, False)

        if i == 1:
            near(0)

    finish(1)
    project_and_send(1)

    copies[9].wait()
    copies[10].wait()

    def entered(i, _):
        @pl.when(i != rank)
        def _():
            pltpu.make_async_copy(in_recv.at[i], in_recv.at[i], inr.at[i]).wait()

        return 0

    lax.fori_loop(0, RANKS, entered, 0)

    def gate_chunk(ci, squares):
        cols = pl.ds(pl.multiple_of(ci * 256, 256), 256)
        enter = jnp.concatenate([in_recv[2 * ci], in_recv[2 * ci + 1]], axis=1)
        second = (expx[BL - 1 : BL, cols] * enter.astype(F32) + s0buf[:, cols]).astype(BF16)
        out = []
        for b, state in enumerate((enter, second)):
            rows = slice(b * BL, (b + 1) * BL)
            value = inner[rows, cols] + expx[rows, cols] * dot(cv[rows, :], state)
            value = value + skx[0:1, cols] * xv[rows, cols].astype(F32)
            gate = gv[rows, cols].astype(F32)
            value = value * (gate / (1.0 + jnp.exp(-gate)))
            inner[rows, cols] = value
            square = value * value
            out.append(squares[b] + (square[:, :128] + square[:, 128:]))
        return tuple(out)

    zero = jnp.zeros((BL, 128), F32)
    squares = lax.fori_loop(0, FEATURES // 256, gate_chunk, (zero, zero))
    factors = [
        lax.rsqrt(jnp.sum(s, axis=1, keepdims=True) * (1.0 / FEATURES) + 1e-05) for s in squares
    ]

    def norm_chunk(ci, _):
        cols = pl.ds(pl.multiple_of(ci * 256, 256), 256)
        for b in range(2):
            rows = slice(b * BL, (b + 1) * BL)
            ssm_v[rows, cols] = (inner[rows, cols] * factors[b] * gnv[:, cols]).astype(BF16)
        return 0

    lax.fori_loop(0, FEATURES // 256, norm_chunk, 0)
    ssm_out = pltpu.make_async_copy(ssm_v, ssm_hbm, out_sem.at[2])
    ssm_out.start()

    near(1)
    last(0)
    last(1)

    for d in range(1, SIDE):
        kv_copy(rank, rank, d - 1).wait_send()
    for xd in range(1, SIDE):

        @pl.when((core == 1) & (xd > x))
        def _():
            kv_copy(rank, rank, 2 + xd).wait_send()

        for yb in range(SIDE):

            @pl.when((core == 0) & (xd > x))
            def _():
                kv_copy(rank, rank, 3 + 4 * (xd - 1) + yb).wait_send()

    for xb in range(SIDE - 1):

        @pl.when((core == 1) & (xb < x))
        def _():
            for d in range(1, SIDE):
                kv_copy(rank, rank, 6 + 3 * xb + d - 1).wait_send()

    def states_left(d, _):
        other = (rank + d) % RANKS
        state_copy(other).wait_send()
        in_copy(other).wait_send()
        return 0

    lax.fori_loop(1, RANKS, states_left, 0)
    for half in range(2):
        for d in range(SIDE):
            xs_copy(half, d).wait_send()
        for way in range(2):
            far_copy(half, way).wait_send()
            near_copy(half, way).wait_send()
    ssm_out.wait()
    mixed_out(0).wait()
    mixed_out(1).wait()


def local(
    queries, keys, values, out_weight, ssm_input, ssm_gate, in_map, out_map, log_decay, skip, norm_gain
):
    anywhere = pl.BlockSpec(memory_space=pl.ANY)
    sem = pltpu.SemaphoreType.DMA
    scratch = [
        pltpu.VMEM((TOK, HEADS * HD), BF16),
        pltpu.VMEM((RANKS, 2, TOK, HD), BF16),
        pltpu.VMEM((HEADS * HD, 8 * WIDE), BF16),
        pltpu.VMEM((TOK, FEATURES), BF16),
        pltpu.VMEM((TOK, FEATURES), BF16),
        pltpu.VMEM((TOK, NS), BF16),
        pltpu.VMEM((TOK, NS), BF16),
        pltpu.VMEM((TOK, MIXERS), F32),
        pltpu.VMEM((1, MIXERS), F32),
        pltpu.VMEM((1, FEATURES), F32),
        pltpu.VMEM((TOK, 128), BF16),
        pltpu.VMEM((2, 128, BL), F32),
        pltpu.VMEM((2, BL, BL), F32),
        pltpu.VMEM((2, NS, BL), BF16),
        pltpu.VMEM((TOK, 128), BF16),
        pltpu.VMEM((TOK, 128), BF16),
        pltpu.VMEM((TOK, FEATURES), F32),
        pltpu.VMEM((8, FEATURES), F32),
        pltpu.VMEM((TOK, FEATURES), F32),
        pltpu.VMEM((NS, FEATURES), F32),
        pltpu.VMEM((RANKS, PIECE, 128), BF16),
        pltpu.VMEM((RANKS, PIECE, 128), BF16),
        pltpu.VMEM((RANKS, NS, 128), BF16),
        pltpu.VMEM((RANKS, NS, 128), BF16),
        pltpu.VMEM((TOK, FEATURES), BF16),
        pltpu.VMEM((HEADS, HALF, 2 * HD), F32),
        pltpu.VMEM((HEADS, HALF, 128), F32),
        pltpu.VMEM((HALF, HEADS * HD), BF16),
        pltpu.VMEM((2, SIDE, HALF, WIDE), F32),
        pltpu.VMEM((2, SIDE, HALF, WIDE), BF16),
        pltpu.VMEM((2, SIDE, HALF, WIDE), BF16),
        pltpu.VMEM((2, 2, HALF // 2, WIDE), BF16),
        pltpu.VMEM((2, 2, HALF // 2, WIDE), BF16),
        pltpu.VMEM((2, 2, HALF, WIDE), BF16),
        pltpu.VMEM((2, 2, HALF, WIDE), BF16),
        pltpu.VMEM((2, HALF, WIDE), BF16),
        sem((11,)),
        sem((16,)),
        sem((RANKS,)),
        sem((RANKS,)),
        sem((RANKS,)),
        sem((RANKS,)),
        sem((RANKS,)),
        sem((2, SIDE)),
        sem((2, SIDE)),
        sem((2, 2)),
        sem((2, 2)),
        sem((2, 2)),
        sem((2, 2)),
        sem((3,)),
    ]
    return pl.pallas_call(
        kernel,
        out_shape=(
            jax.ShapeDtypeStruct((TOK, WIDE), BF16),
            jax.ShapeDtypeStruct((TOK, FEATURES), BF16),
        ),
        in_specs=[anywhere] * 11,
        out_specs=(anywhere, anywhere),
        scratch_shapes=scratch,
        compiler_params=pltpu.CompilerParams(
            collective_id=0, has_side_effects=True, vmem_limit_bytes=60 * 1024 * 1024
        ),
        cost_estimate=pl.CostEstimate(
            flops=9_000_000_000, bytes_accessed=24_000_000, transcendentals=9_000_000
        ),
    )(
        queries, keys, values, out_weight, ssm_input, ssm_gate, in_map, out_map, log_decay,
        skip.reshape(1, MIXERS), norm_gain.reshape(1, FEATURES),
    )


def solution(mesh):
    in_specs = (
        P("ctx", "tp"),
        P("ctx", "tp"),
        P("ctx", "tp"),
        P("tp", None),
        P("ctx", "tp"),
        P("ctx", "tp"),
        P("ctx", "tp"),
        P("ctx", "tp"),
        P("ctx", "tp"),
        P("tp"),
        P("tp"),
    )
    out_specs = (P("ctx", "tp"), P("ctx", "tp"))
    return jax.shard_map(local, mesh=mesh, in_specs=in_specs, out_specs=out_specs, check_vma=False)
```

time: 275 us -> 84.8 us (0.31)
  the two profiles are of different devices: /device:TPU:0 before, /device:TPU:6 now
where the time goes in v1:
time: 84.8 us; the launch traced here: 84.6 us
  Pallas kernels  78.2 us (92%)
  local copies, waits for them, and re-layouts  5.68 us (7%)
    pallas_call x1, Pallas kernels, local(): pl.pallas_call(kernel, out_shape=(jax.ShapeDtypeStruct((TOK, WIDE), BF16)...  78.2 us
    unnamed x3, local copies, waits for them, and re-layouts  5.68 us

profile of v1, /device:TPU:6, one launch (start us, length us, event | category | flops | bytes accessed | tf_op | source)
XLA Modules:
  0.0 84.6 jit_solution(10120604208474967493)
XLA Ops:
  0.6 1.5 %copy.13.ld_hbm = f32[256,32]{1,0:T(8,128)} copy(f32[256,32]{0,1:T(8,128)} %param.19) | data formatting | bytes 65536 | tf_op args[8]
  2.1 78.2 %shard_map.122 = (bf16[256,1024]{1,0:T(8,128)(2,1)}, bf16[256,2048]{1,0:T(8,128)(2,1)}) custom-call(bf16[256,1024]{1,0:T(8,128)(2,1)} %q_hbm.1, bf16[256,128]{1,0:T(8,128)(2,1)} %k_hbm.1, bf16[256,128]{1,0:T(8,128)(2,1)} %v_hbm.1, bf16[1024,8192]{1,0:T(8,128)(2,1)} %w_hbm.1, bf16[256,2048]{1,0:T(8,128)(2,1)} %x_hbm.1, bf16[256,2048]{1,0:T(8,128)(2,1)} %g_hbm.1, ...), custom_call_target="tpu_custom_call" | custom-call | flops 8999999488 | bytes 24000000 | tf_op jit(solution)/shard_map/pallas_call | solution.py:578
  80.4 1.9 %copy.16 = bf16[256,1024]{1,0:T(8,128)(2,1)} copy(bf16[256,1024]{1,0:T(8,128)(2,1)} %get-tuple-element.4) | data formatting | bytes 1048576
  82.3 2.3 %copy.17 = bf16[256,2048]{1,0:T(8,128)(2,1)} copy(bf16[256,2048]{1,0:T(8,128)(2,1)} %get-tuple-element.5) | data formatting | bytes 2097152

commit v2 on v1

--- a/solution.py
+++ b/solution.py
@@ -118,25 +118,32 @@
             device_id_type=MESH,
         )
 
+    def row_needs(block_y, dest_y):
+        return (dest_y > block_y) | ((core == 0) & (x < SIDE - 1))
+
     copies[0].wait()
     copies[1].wait()
+    for xd in range(SIDE - 1, 0, -1):
+
+        @pl.when(xd > x)
+        def _():
+            kv_copy(rank, SIDE * xd + y, 2 + xd).start()
+
     for d in range(1, SIDE):
-        kv_copy(rank, SIDE * x + (y + d) % SIDE, d - 1).start()
-    for xd in range(1, SIDE):
-
-        @pl.when((core == 1) & (xd > x))
-        def _():
-            kv_copy(rank, SIDE * xd + y, 2 + xd).start()
+        yd = (y + d) % SIDE
+
+        @pl.when(row_needs(y, yd))
+        def _():
+            kv_copy(rank, SIDE * x + yd, d - 1).start()
 
     copies[2].wait()
     copies[3].wait()
     repeat = (iota((MIXERS, 128), 1) % MIXERS == iota((MIXERS, 128), 0)).astype(F32).astype(BF16)
     lower = (iota((BL, BL), 0) >= iota((BL, BL), 1)).astype(F32).astype(BF16)
-    decays = [dot(part, repeat) for part in split3(ldv[...])]
-    decays = (decays[0] + decays[1]) + decays[2]
+    decays = jnp.concatenate([ldv[...]] * 4, axis=0)
     for b in range(2):
         rows = slice(b * BL, (b + 1) * BL)
-        cum = [dot(lower, part) for part in split3(decays[rows])]
+        cum = [dot(lower, part) for part in split3(decays[:, rows].T)]
         cum = (cum[0] + cum[1]) + cum[2]
         cumsplit[rows, :] = lane_split(cum)
         cum_rows[b] = cum.T
@@ -186,19 +193,24 @@
         state_copy((rank + d) % RANKS).start()
         return 0
 
-    lax.fori_loop(1, RANKS, send_state, 0)
-    st_recv[rank] = st_send[rank]
-
     for d in range(1, SIDE):
-        kv_copy(SIDE * x + (y + d) % SIDE, rank, 0).wait_recv()
-    for xd in range(1, SIDE):
-        for yb in range(SIDE):
+        yb = (y + d) % SIDE
+
+        @pl.when(row_needs(yb, y))
+        def _():
+            kv_copy(SIDE * x + yb, rank, 0).wait_recv()
+
+        @pl.when(jnp.logical_not(row_needs(yb, y)))
+        def _():
+            kv[SIDE * x + yb, 1] = jnp.zeros((TOK, HD), BF16)
+
+        for xd in range(SIDE - 1, 0, -1):
 
             @pl.when((core == 0) & (xd > x))
             def _():
-                kv_copy(SIDE * x + yb, SIDE * xd + y, 3 + 4 * (xd - 1) + yb).start()
-
-    for xb in range(SIDE - 1):
+                kv_copy(SIDE * x + yb, SIDE * xd + y, 6 + 3 * (xd - 1) + d - 1).start()
+
+    for xb in range(SIDE - 2, -1, -1):
 
         @pl.when((core == 1) & (xb < x))
         def _():
@@ -254,38 +266,52 @@
         tail = st_recv[i, NS:, :].astype(F32)
         return (tail[0:1] + tail[1:2]) * before + st_recv[i, :NS, :].astype(F32)
 
-    lax.fori_loop(0, RANKS, prefix, jnp.zeros((NS, 128), F32))
-    in_recv[rank] = in_send[rank]
-
     copies[7].wait()
     ones = jnp.ones((WIDE, HD), BF16)
 
     def absorb(half, row_index, first):
-        def pair(hp, _):
-            for u in range(2):
-                h = 2 * hp + u
-                q = qv[half * HALF : (half + 1) * HALF, pl.ds(pl.multiple_of(h * HD, HD), HD)]
-                keys = kv[pl.ds(SIDE * row_index, SIDE), 0].reshape(WIDE, HD)
-                values = kv[pl.ds(SIDE * row_index, SIDE), 1].reshape(WIDE, HD)
-                values = jnp.concatenate([values, ones], axis=1)
-                scores = dot_t(q, keys)
-                if first:
-                    place = iota((HALF, WIDE), 0) + (y * TOK + half * HALF)
-                    scores = jnp.where(iota((HALF, WIDE), 1) <= place, scores, -1e30)
-                    new = jnp.max(scores, axis=1, keepdims=True)
-                else:
-                    old = top[h, :, 0:1]
-                    new = jnp.maximum(old, jnp.max(scores, axis=1, keepdims=True))
-                weights = jnp.exp2(scores * SCORE_SCALE - new * SCORE_SCALE).astype(BF16)
-                add = dot(weights, values)
-                if first:
-                    acc[h] = add
-                else:
-                    acc[h] = acc[h] * jnp.exp2((old - new) * SCORE_SCALE) + add
-                top[h] = jnp.broadcast_to(new, (HALF, 128))
-            return 0
-
-        lax.fori_loop(0, HEADS // 2, pair, 0)
+        chunk = kv[pl.ds(SIDE * row_index, SIDE)]
+        keys = chunk[:, 0].reshape(WIDE, HD)
+        values = jnp.concatenate([chunk[:, 1].reshape(WIDE, HD), ones], axis=1)
+        lanes = [slice(j * 128, (j + 1) * 128) for j in range(WIDE // 128)]
+
+        def score(h):
+            q = qv[half * HALF : (half + 1) * HALF, h * HD : (h + 1) * HD]
+            scores = dot_t(q, keys)
+            if first:
+                place = iota((HALF, WIDE), 0) + (y * TOK + half * HALF)
+                scores = jnp.where(iota((HALF, WIDE), 1) <= place, scores, -1e30)
+            return scores
+
+        def weigh(h, scores):
+            high = scores[:, lanes[0]]
+            for part in lanes[1:]:
+                high = jnp.maximum(high, scores[:, part])
+            new = jnp.broadcast_to(jnp.max(high, axis=1, keepdims=True), (HALF, 128))
+            shrink = None
+            if not first:
+                old = top[h]
+                new = jnp.maximum(old, new)
+                shrink = jnp.exp2((old - new) * SCORE_SCALE)
+            top[h] = new
+            new = new * SCORE_SCALE
+            weights = [jnp.exp2(scores[:, p] * SCORE_SCALE - new).astype(BF16) for p in lanes]
+            return jnp.concatenate(weights, axis=1), shrink
+
+        def add_up(h, weights, shrink):
+            add = dot(weights, values)
+            if not first:
+                add = acc[h] * jnp.concatenate([shrink, shrink], axis=1) + add
+            acc[h] = add
+
+        scores, weights = {}, {}
+        for step in range(HEADS + 2):
+            if step < HEADS:
+                scores[step] = score(step)
+            if 0 <= step - 1 < HEADS:
+                weights[step - 1] = weigh(step - 1, scores.pop(step - 1))
+            if 0 <= step - 2:
+                add_up(step - 2, *weights.pop(step - 2))
 
     def wait_row(row_index):
         for yb in range(SIDE):
@@ -305,9 +331,6 @@
     def project(block):
         cols = pl.ds(pl.multiple_of(block * WIDE, WIDE), WIDE)
         return dot(att[...], wv[:, cols])
-
-    def far_first(i):
-        return (2 + i) % SIDE
 
     def xs_copy(half, d):
         return pltpu.make_async_remote_copy(
@@ -319,85 +342,98 @@
             device_id_type=MESH,
         )
 
-    def ring_copy(src, dst, send, recv, half, way):
+    def far_copy(half, way):
         return pltpu.make_async_remote_copy(
-            src_ref=src.at[half, way],
-            dst_ref=dst.at[half, way],
-            send_sem=send.at[half, way],
-            recv_sem=recv.at[half, way],
+            src_ref=fs.at[half, way],
+            dst_ref=fr.at[half, way],
+            send_sem=fss.at[half, way],
+            recv_sem=fsr.at[half, way],
             device_id=(rank, up if way == 0 else down),
             device_id_type=MESH,
         )
 
-    def far_copy(half, way):
-        return ring_copy(fs, fr, fss, fsr, half, way)
-
-    def near_copy(half, way):
-        return ring_copy(ns, nr, nss, nsr, half, way)
-
+    def near_copy(half, way, quarter):
+        return pltpu.make_async_remote_copy(
+            src_ref=ns.at[half, way, quarter],
+            dst_ref=nr.at[half, way, quarter],
+            send_sem=nss.at[half, way, quarter],
+            recv_sem=nsr.at[half, way, quarter],
+            device_id=(rank, up if way == 0 else down),
+            device_id_type=MESH,
+        )
+
+    near_of = (1, 3)
     STEP = 32
 
+    def for_partner(half, d):
+        xs[half, d] = project(2 * ((z + d) % SIDE) + 1 - core).astype(BF16)
+        xs_copy(half, d).start()
+
+    def for_own(half, d):
+        own[half, d] = project(2 * ((z + d) % SIDE) + core)
+
+    def near_part(half, way, quarter, with_far):
+        d = near_of[way]
+
+        def near_sum(t, _):
+            at = pl.ds(pl.multiple_of(t * STEP, STEP), STEP)
+            rows = pl.ds(pl.multiple_of(64 * quarter + t * STEP, STEP), STEP)
+            total = own[half, d, rows, :] + xr[half, d, rows, :].astype(F32)
+            if with_far:
+                total = total + fr[half, way, at, :].astype(F32)
+            ns[half, way, quarter, at, :] = total.astype(BF16)
+            return 0
+
+        lax.fori_loop(0, 64 // STEP, near_sum, 0)
+        near_copy(half, way, quarter).start()
+
     def project_and_send(half):
-        def for_partner(i, _):
-            d = far_first(i)
-            xs[half, d] = project(2 * ((z + d) % SIDE) + 1 - core).astype(BF16)
-            xs_copy(half, d).start()
-            return 0
-
-        def for_own(i, _):
-            d = far_first(i)
-            own[half, d] = project(2 * ((z + d) % SIDE) + core)
-            return 0
-
-        lax.fori_loop(0, SIDE, for_partner, 0)
-        for_own(0, 0)
+        for_partner(half, 2)
+        for_own(half, 2)
+        for_partner(half, 1)
+        for_partner(half, 3)
         xs_copy(half, 2).wait_recv()
         for way in range(2):
 
             def far_sum(t, _):
+                at = pl.ds(pl.multiple_of(t * STEP, STEP), STEP)
                 rows = pl.ds(pl.multiple_of(64 * way + t * STEP, STEP), STEP)
-                fs[half, way, pl.ds(pl.multiple_of(t * STEP, STEP), STEP), :] = (
+                fs[half, way, at, :] = (
                     own[half, 2, rows, :] + xr[half, 2, rows, :].astype(F32)
                 ).astype(BF16)
                 return 0
 
             lax.fori_loop(0, 64 // STEP, far_sum, 0)
             far_copy(half, way).start()
-        lax.fori_loop(1, SIDE, for_own, 0)
+        for way in range(2):
+            d = near_of[way]
+            for_own(half, d)
+            xs_copy(half, d).wait_recv()
+            near_part(half, way, 1 - way, False)
+        for_partner(half, 0)
+        for_own(half, 0)
 
     def near(half):
         for way in range(2):
-            d = 1 if way == 0 else 3
-            xs_copy(half, d).wait_recv()
             far_copy(half, way).wait_recv()
-
-            def near_sum(t, _):
-                for has_far in (True, False):
-                    start = 64 * way if has_far else 64 - 64 * way
-                    rows = pl.ds(pl.multiple_of(start + t * STEP, STEP), STEP)
-                    total = own[half, d, rows, :] + xr[half, d, rows, :].astype(F32)
-                    if has_far:
-                        far = fr[half, way, pl.ds(pl.multiple_of(t * STEP, STEP), STEP), :]
-                        total = total + far.astype(F32)
-                    ns[half, way, rows, :] = total.astype(BF16)
-                return 0
-
-            lax.fori_loop(0, 64 // STEP, near_sum, 0)
-            near_copy(half, way).start()
+            near_part(half, way, way, True)
 
     def last(half):
         xs_copy(half, 0).wait_recv()
-        near_copy(half, 0).wait_recv()
-        near_copy(half, 1).wait_recv()
-
-        def last_sum(t, _):
-            rows = pl.ds(pl.multiple_of(t * STEP, STEP), STEP)
-            total = own[half, 0, rows, :] + xr[half, 0, rows, :].astype(F32)
-            total = total + nr[half, 0, rows, :].astype(F32) + nr[half, 1, rows, :].astype(F32)
-            mixed_v[half, rows, :] = total.astype(BF16)
-            return 0
-
-        lax.fori_loop(0, HALF // STEP, last_sum, 0)
+        for quarter in range(2):
+            near_copy(half, 0, quarter).wait_recv()
+            near_copy(half, 1, quarter).wait_recv()
+
+            def last_sum(t, _):
+                at = pl.ds(pl.multiple_of(t * STEP, STEP), STEP)
+                rows = pl.ds(pl.multiple_of(64 * quarter + t * STEP, STEP), STEP)
+                total = own[half, 0, rows, :] + xr[half, 0, rows, :].astype(F32)
+                total = total + nr[half, 0, quarter, at, :].astype(F32)
+                total = total + nr[half, 1, quarter, at, :].astype(F32)
+                mixed_v[half, rows, :] = total.astype(BF16)
+                return 0
+
+            lax.fori_loop(0, 64 // STEP, last_sum, 0)
         mixed_out(half).start()
 
     def mixed_out(half):
@@ -406,29 +442,40 @@
         )
 
     absorb(0, x, True)
-    for i in range(1, SIDE):
-
-        @pl.when(i <= x)
-        def _():
-            wait_row(x - i)
-            absorb(0, x - i, False)
-
+
+    def earlier_row(i, _):
+        wait_row(x - i)
+        absorb(0, x - i, False)
+        return 0
+
+    lax.fori_loop(1, x + 1, earlier_row, 0)
     finish(0)
     copies[8].wait()
     project_and_send(0)
+    lax.fori_loop(1, RANKS, send_state, 0)
+    st_recv[rank] = st_send[rank]
 
     absorb(1, x, True)
-    for i in range(1, SIDE):
-
-        @pl.when(i <= x)
-        def _():
-            absorb(1, x - i, False)
-
-        if i == 1:
+
+    @pl.when(x == 0)
+    def _():
+        near(0)
+
+    def earlier_row_again(i, _):
+        absorb(1, x - i, False)
+
+        @pl.when(i == 1)
+        def _():
             near(0)
 
+        return 0
+
+    lax.fori_loop(1, x + 1, earlier_row_again, 0)
     finish(1)
+    lax.fori_loop(0, RANKS, prefix, jnp.zeros((NS, 128), F32))
+    in_recv[rank] = in_send[rank]
     project_and_send(1)
+    near(1)
 
     copies[9].wait()
     copies[10].wait()
@@ -475,23 +522,26 @@
     ssm_out = pltpu.make_async_copy(ssm_v, ssm_hbm, out_sem.at[2])
     ssm_out.start()
 
-    near(1)
     last(0)
     last(1)
 
     for d in range(1, SIDE):
-        kv_copy(rank, rank, d - 1).wait_send()
+
+        @pl.when(row_needs(y, (y + d) % SIDE))
+        def _():
+            kv_copy(rank, rank, d - 1).wait_send()
+
     for xd in range(1, SIDE):
 
-        @pl.when((core == 1) & (xd > x))
+        @pl.when(xd > x)
         def _():
             kv_copy(rank, rank, 2 + xd).wait_send()
 
-        for yb in range(SIDE):
+        for d in range(1, SIDE):
 
             @pl.when((core == 0) & (xd > x))
             def _():
-                kv_copy(rank, rank, 3 + 4 * (xd - 1) + yb).wait_send()
+                kv_copy(rank, rank, 6 + 3 * (xd - 1) + d - 1).wait_send()
 
     for xb in range(SIDE - 1):
 
@@ -512,10 +562,32 @@
             xs_copy(half, d).wait_send()
         for way in range(2):
             far_copy(half, way).wait_send()
-            near_copy(half, way).wait_send()
+            near_copy(half, way, 0).wait_send()
+            near_copy(half, way, 1).wait_send()
     ssm_out.wait()
     mixed_out(0).wait()
     mixed_out(1).wait()
+
+
+def place(a, b, a_out, b_out, a_v, b_v, sem_in, sem_out):
+    parts = []
+    for source, stage, target in ((b, b_v, b_out), (a, a_v, a_out)):
+        for part in range(2):
+            rows = slice(part * HALF, (part + 1) * HALF)
+            n = len(parts)
+            parts.append(
+                (
+                    pltpu.make_async_copy(source.at[rows], stage.at[rows], sem_in.at[n]),
+                    pltpu.make_async_copy(stage.at[rows], target.at[rows], sem_out.at[n]),
+                )
+            )
+    for arrive, _ in parts:
+        arrive.start()
+    for arrive, leave in parts:
+        arrive.wait()
+        leave.start()
+    for _, leave in parts:
+        leave.wait()
 
 
 def local(
@@ -531,7 +603,7 @@
         pltpu.VMEM((TOK, FEATURES), BF16),
         pltpu.VMEM((TOK, NS), BF16),
         pltpu.VMEM((TOK, NS), BF16),
-        pltpu.VMEM((TOK, MIXERS), F32),
+        pltpu.VMEM((MIXERS, TOK), F32),
         pltpu.VMEM((1, MIXERS), F32),
         pltpu.VMEM((1, FEATURES), F32),
         pltpu.VMEM((TOK, 128), BF16),
@@ -557,8 +629,8 @@
         pltpu.VMEM((2, SIDE, HALF, WIDE), BF16),
         pltpu.VMEM((2, 2, HALF // 2, WIDE), BF16),
         pltpu.VMEM((2, 2, HALF // 2, WIDE), BF16),
-        pltpu.VMEM((2, 2, HALF, WIDE), BF16),
-        pltpu.VMEM((2, 2, HALF, WIDE), BF16),
+        pltpu.VMEM((2, 2, 2, HALF // 2, WIDE), BF16),
+        pltpu.VMEM((2, 2, 2, HALF // 2, WIDE), BF16),
         pltpu.VMEM((2, HALF, WIDE), BF16),
         sem((11,)),
         sem((16,)),
@@ -571,11 +643,11 @@
         sem((2, SIDE)),
         sem((2, 2)),
         sem((2, 2)),
-        sem((2, 2)),
-        sem((2, 2)),
+        sem((2, 2, 2)),
+        sem((2, 2, 2)),
         sem((3,)),
     ]
-    return pl.pallas_call(
+    mixed, ssm_out = pl.pallas_call(
         kernel,
         out_shape=(
             jax.ShapeDtypeStruct((TOK, WIDE), BF16),
@@ -591,9 +663,25 @@
             flops=9_000_000_000, bytes_accessed=24_000_000, transcendentals=9_000_000
         ),
     )(
-        queries, keys, values, out_weight, ssm_input, ssm_gate, in_map, out_map, log_decay,
+        queries, keys, values, out_weight, ssm_input, ssm_gate, in_map, out_map, log_decay.T,
         skip.reshape(1, MIXERS), norm_gain.reshape(1, FEATURES),
     )
+    return pl.pallas_call(
+        place,
+        out_shape=(
+            jax.ShapeDtypeStruct((TOK, WIDE), BF16),
+            jax.ShapeDtypeStruct((TOK, FEATURES), BF16),
+        ),
+        in_specs=[anywhere] * 2,
+        out_specs=(anywhere, anywhere),
+        scratch_shapes=[
+            pltpu.VMEM((TOK, WIDE), BF16),
+            pltpu.VMEM((TOK, FEATURES), BF16),
+            sem((4,)),
+            sem((4,)),
+        ],
+        compiler_params=pltpu.CompilerParams(vmem_limit_bytes=60 * 1024 * 1024),
+    )(mixed, ssm_out)
 
 
 def solution(mesh):

time: 84.8 us -> 64 us (0.75)
  the two profiles are of different devices: /device:TPU:6 before, /device:TPU:24 now
where the time goes in v2:
time: 64 us; the launch traced here: 63.9 us
  Pallas kernels  63.1 us (99%)
  between operations  0.8 us (1%)
    pallas_call x1, Pallas kernels, local(): pl.pallas_call(kernel, out_shape=(jax.ShapeDtypeStruct((TOK, WIDE), BF16)...  60.9 us
    pallas_call x1, Pallas kernels, local(): pl.pallas_call(place, out_shape=(jax.ShapeDtypeStruct((TOK, WIDE), BF16),...  2.24 us

profile of v2, /device:TPU:24, one launch (start us, length us, event | category | flops | bytes accessed | tf_op | source)
XLA Modules:
  0.0 63.9 jit_solution(5935445548447715468)
XLA Ops:
  0.6 60.9 %shard_map.122 = (bf16[256,1024]{1,0:T(8,128)(2,1)}, bf16[256,2048]{1,0:T(8,128)(2,1)}) custom-call(bf16[256,1024]{1,0:T(8,128)(2,1)} %q_hbm.1, bf16[256,128]{1,0:T(8,128)(2,1)} %k_hbm.1, bf16[256,128]{1,0:T(8,128)(2,1)} %v_hbm.1, bf16[1024,8192]{1,0:T(8,128)(2,1)} %w_hbm.1, bf16[256,2048]{1,0:T(8,128)(2,1)} %x_hbm.1, bf16[256,2048]{1,0:T(8,128)(2,1)} %g_hbm.1, ...), custom_call_target="tpu_custom_call" | custom-call | flops 8999999488 | bytes 24000000 | tf_op jit(solution)/shard_map/pallas_call | solution.py:650
  61.5 2.2 %shard_map.123 = (bf16[256,1024]{1,0:T(8,128)(2,1)}, bf16[256,2048]{1,0:T(8,128)(2,1)}) custom-call(bf16[256,1024]{1,0:T(8,128)(2,1)} %get-tuple-element.4.a, bf16[256,2048]{1,0:T(8,128)(2,1)} %get-tuple-element.5.b), custom_call_target="tpu_custom_call" | custom-call | tf_op jit(solution)/shard_map/pallas_call | solution.py:669

commit v3 on v2

--- a/solution.py
+++ b/solution.py
@@ -155,6 +155,31 @@
     copies[5].wait()
     for b in range(2):
         bt[b] = bv[b * BL : (b + 1) * BL, :].astype(F32).T.astype(BF16)
+
+    for d in range(1, SIDE):
+        yb = (y + d) % SIDE
+
+        @pl.when(row_needs(yb, y))
+        def _():
+            kv_copy(SIDE * x + yb, rank, 0).wait_recv()
+
+        @pl.when(jnp.logical_not(row_needs(yb, y)))
+        def _():
+            kv[SIDE * x + yb, 1] = jnp.zeros((TOK, HD), BF16)
+
+        for xd in range(SIDE - 1, 0, -1):
+
+            @pl.when((core == 0) & (xd > x))
+            def _():
+                kv_copy(SIDE * x + yb, SIDE * xd + y, 6 + 3 * (xd - 1) + d - 1).start()
+
+    for xb in range(SIDE - 2, -1, -1):
+
+        @pl.when((core == 1) & (xb < x))
+        def _():
+            kv_copy(SIDE * xb + y, rank, 0).wait_recv()
+            for d in range(1, SIDE):
+                kv_copy(SIDE * xb + y, SIDE * x + (y + d) % SIDE, 6 + 3 * xb + d - 1).start()
 
     def state_chunk(ci, _):
         cols = pl.ds(pl.multiple_of(ci * 256, 256), 256)
@@ -177,7 +202,7 @@
             st_send[2 * ci + u, NS:, :] = tail[:, u * 128 : (u + 1) * 128]
         return 0
 
-    lax.fori_loop(0, FEATURES // 256, state_chunk, 0)
+    lax.fori_loop(0, FEATURES // 256, state_chunk, 0, unroll=4)
 
     def state_copy(piece):
         return pltpu.make_async_remote_copy(
@@ -192,31 +217,6 @@
     def send_state(d, _):
         state_copy((rank + d) % RANKS).start()
         return 0
-
-    for d in range(1, SIDE):
-        yb = (y + d) % SIDE
-
-        @pl.when(row_needs(yb, y))
-        def _():
-            kv_copy(SIDE * x + yb, rank, 0).wait_recv()
-
-        @pl.when(jnp.logical_not(row_needs(yb, y)))
-        def _():
-            kv[SIDE * x + yb, 1] = jnp.zeros((TOK, HD), BF16)
-
-        for xd in range(SIDE - 1, 0, -1):
-
-            @pl.when((core == 0) & (xd > x))
-            def _():
-                kv_copy(SIDE * x + yb, SIDE * xd + y, 6 + 3 * (xd - 1) + d - 1).start()
-
-    for xb in range(SIDE - 2, -1, -1):
-
-        @pl.when((core == 1) & (xb < x))
-        def _():
-            kv_copy(SIDE * xb + y, rank, 0).wait_recv()
-            for d in range(1, SIDE):
-                kv_copy(SIDE * xb + y, SIDE * x + (y + d) % SIDE, 6 + 3 * xb + d - 1).start()
 
     copies[6].wait()
     for b in range(2):
@@ -240,7 +240,6 @@
             inner[rows, cols] = dot(jnp.concatenate(mixing, axis=1), both)
         return 0
 
-    lax.fori_loop(0, MIXERS // 2, inner_pair, 0)
 
     def in_copy(dest):
         return pltpu.make_async_remote_copy(
@@ -269,31 +268,32 @@
     copies[7].wait()
     ones = jnp.ones((WIDE, HD), BF16)
 
-    def absorb(half, row_index, first):
+    def absorb(low, count, row_index, first):
+        picked = slice(low, low + count)
         chunk = kv[pl.ds(SIDE * row_index, SIDE)]
         keys = chunk[:, 0].reshape(WIDE, HD)
         values = jnp.concatenate([chunk[:, 1].reshape(WIDE, HD), ones], axis=1)
         lanes = [slice(j * 128, (j + 1) * 128) for j in range(WIDE // 128)]
 
         def score(h):
-            q = qv[half * HALF : (half + 1) * HALF, h * HD : (h + 1) * HD]
+            q = qv[picked, h * HD : (h + 1) * HD]
             scores = dot_t(q, keys)
             if first:
-                place = iota((HALF, WIDE), 0) + (y * TOK + half * HALF)
-                scores = jnp.where(iota((HALF, WIDE), 1) <= place, scores, -1e30)
+                place = iota((count, WIDE), 0) + (y * TOK + low)
+                scores = jnp.where(iota((count, WIDE), 1) <= place, scores, -1e30)
             return scores
 
         def weigh(h, scores):
             high = scores[:, lanes[0]]
             for part in lanes[1:]:
                 high = jnp.maximum(high, scores[:, part])
-            new = jnp.broadcast_to(jnp.max(high, axis=1, keepdims=True), (HALF, 128))
+            new = jnp.broadcast_to(jnp.max(high, axis=1, keepdims=True), (count, 128))
             shrink = None
             if not first:
-                old = top[h]
+                old = top[h, picked]
                 new = jnp.maximum(old, new)
                 shrink = jnp.exp2((old - new) * SCORE_SCALE)
-            top[h] = new
+            top[h, picked] = new
             new = new * SCORE_SCALE
             weights = [jnp.exp2(scores[:, p] * SCORE_SCALE - new).astype(BF16) for p in lanes]
             return jnp.concatenate(weights, axis=1), shrink
@@ -301,8 +301,8 @@
         def add_up(h, weights, shrink):
             add = dot(weights, values)
             if not first:
-                add = acc[h] * jnp.concatenate([shrink, shrink], axis=1) + add
-            acc[h] = add
+                add = acc[h, picked] * jnp.concatenate([shrink, shrink], axis=1) + add
+            acc[h, picked] = add
 
         scores, weights = {}, {}
         for step in range(HEADS + 2):
@@ -322,7 +322,7 @@
 
     def finish(half):
         def one(h, _):
-            a = acc[h]
+            a = acc[h, half * HALF : (half + 1) * HALF]
             att[:, pl.ds(pl.multiple_of(h * HD, HD), HD)] = (a[:, :HD] / a[:, HD:]).astype(BF16)
             return 0
 
@@ -387,11 +387,14 @@
         lax.fori_loop(0, 64 // STEP, near_sum, 0)
         near_copy(half, way, quarter).start()
 
-    def project_and_send(half):
+    def project_first(half):
         for_partner(half, 2)
         for_own(half, 2)
         for_partner(half, 1)
         for_partner(half, 3)
+        for_own(half, 1)
+
+    def far(half):
         xs_copy(half, 2).wait_recv()
         for way in range(2):
 
@@ -405,15 +408,18 @@
 
             lax.fori_loop(0, 64 // STEP, far_sum, 0)
             far_copy(half, way).start()
-        for way in range(2):
-            d = near_of[way]
-            for_own(half, d)
-            xs_copy(half, d).wait_recv()
-            near_part(half, way, 1 - way, False)
+
+    def project_rest(half):
+        for_own(half, 3)
         for_partner(half, 0)
         for_own(half, 0)
 
-    def near(half):
+    def near_alone(half):
+        for way in range(2):
+            xs_copy(half, near_of[way]).wait_recv()
+            near_part(half, way, 1 - way, False)
+
+    def near_with_far(half):
         for way in range(2):
             far_copy(half, way).wait_recv()
             near_part(half, way, way, True)
@@ -441,41 +447,64 @@
             mixed_v.at[half], mixed_hbm.at[half * HALF : (half + 1) * HALF], out_sem.at[half]
         )
 
-    absorb(0, x, True)
+    @pl.when(x > 0)
+    def _():
+        absorb(0, TOK, x, True)
 
     def earlier_row(i, _):
         wait_row(x - i)
-        absorb(0, x - i, False)
+        absorb(0, TOK, x - i, False)
         return 0
 
-    lax.fori_loop(1, x + 1, earlier_row, 0)
-    finish(0)
+    lax.fori_loop(1, x, earlier_row, 0)
+
+    @pl.when(x > 0)
+    def _():
+        wait_row(0)
+
+    @pl.when(x == SIDE - 1)
+    def _():
+        lax.fori_loop(1, RANKS, send_state, 0)
+
+    def last_row(half):
+        @pl.when(x == 0)
+        def _():
+            absorb(half * HALF, HALF, 0, True)
+
+        @pl.when(x > 0)
+        def _():
+            absorb(half * HALF, HALF, 0, False)
+
+        finish(half)
+
+    last_row(0)
     copies[8].wait()
-    project_and_send(0)
-    lax.fori_loop(1, RANKS, send_state, 0)
+    project_first(0)
+    far(0)
+    project_rest(0)
+
+    @pl.when(x < SIDE - 1)
+    def _():
+        lax.fori_loop(1, RANKS, send_state, 0)
+
     st_recv[rank] = st_send[rank]
-
-    absorb(1, x, True)
-
-    @pl.when(x == 0)
-    def _():
-        near(0)
-
-    def earlier_row_again(i, _):
-        absorb(1, x - i, False)
-
-        @pl.when(i == 1)
-        def _():
-            near(0)
-
-        return 0
-
-    lax.fori_loop(1, x + 1, earlier_row_again, 0)
-    finish(1)
+    for way in range(2):
+        far_copy(0, way).wait_send()
+    near_alone(0)
+
+    last_row(1)
+    near_with_far(0)
+    project_first(1)
+    far(1)
+    project_rest(1)
+    near_alone(1)
     lax.fori_loop(0, RANKS, prefix, jnp.zeros((NS, 128), F32))
     in_recv[rank] = in_send[rank]
-    project_and_send(1)
-    near(1)
+    lax.fori_loop(0, MIXERS // 2, inner_pair, 0, unroll=4)
+    last(0)
+    near_with_far(1)
+    for way in range(2):
+        far_copy(1, way).wait_send()
 
     copies[9].wait()
     copies[10].wait()
@@ -506,7 +535,7 @@
         return tuple(out)
 
     zero = jnp.zeros((BL, 128), F32)
-    squares = lax.fori_loop(0, FEATURES // 256, gate_chunk, (zero, zero))
+    squares = lax.fori_loop(0, FEATURES // 256, gate_chunk, (zero, zero), unroll=4)
     factors = [
         lax.rsqrt(jnp.sum(s, axis=1, keepdims=True) * (1.0 / FEATURES) + 1e-05) for s in squares
     ]
@@ -518,11 +547,9 @@
             ssm_v[rows, cols] = (inner[rows, cols] * factors[b] * gnv[:, cols]).astype(BF16)
         return 0
 
-    lax.fori_loop(0, FEATURES // 256, norm_chunk, 0)
+    lax.fori_loop(0, FEATURES // 256, norm_chunk, 0, unroll=4)
     ssm_out = pltpu.make_async_copy(ssm_v, ssm_hbm, out_sem.at[2])
     ssm_out.start()
-
-    last(0)
     last(1)
 
     for d in range(1, SIDE):
@@ -561,7 +588,6 @@
         for d in range(SIDE):
             xs_copy(half, d).wait_send()
         for way in range(2):
-            far_copy(half, way).wait_send()
             near_copy(half, way, 0).wait_send()
             near_copy(half, way, 1).wait_send()
     ssm_out.wait()
@@ -621,8 +647,8 @@
         pltpu.VMEM((RANKS, NS, 128), BF16),
         pltpu.VMEM((RANKS, NS, 128), BF16),
         pltpu.VMEM((TOK, FEATURES), BF16),
-        pltpu.VMEM((HEADS, HALF, 2 * HD), F32),
-        pltpu.VMEM((HEADS, HALF, 128), F32),
+        pltpu.VMEM((HEADS, TOK, 2 * HD), F32),
+        pltpu.VMEM((HEADS, TOK, 128), F32),
         pltpu.VMEM((HALF, HEADS * HD), BF16),
         pltpu.VMEM((2, SIDE, HALF, WIDE), F32),
         pltpu.VMEM((2, SIDE, HALF, WIDE), BF16),

time: 64 us -> 58 us (0.906)
  the two profiles are of different devices: /device:TPU:24 before, /device:TPU:0 now
where the time goes in v3:
time: 58 us; the launch traced here: 57.1 us
  Pallas kernels  56.3 us (97%)
  between operations  0.8 us (1%)
    pallas_call x1, Pallas kernels, local(): pl.pallas_call(kernel, out_shape=(jax.ShapeDtypeStruct((TOK, WIDE), BF16)...  54.1 us
    pallas_call x1, Pallas kernels, local(): pl.pallas_call(place, out_shape=(jax.ShapeDtypeStruct((TOK, WIDE), BF16),...  2.24 us

profile of v3, /device:TPU:0, one launch (start us, length us, event | category | flops | bytes accessed | tf_op | source)
XLA Modules:
  0.0 57.1 jit_solution(4517615354060780903)
XLA Ops:
  0.6 54.1 %shard_map.122 = (bf16[256,1024]{1,0:T(8,128)(2,1)}, bf16[256,2048]{1,0:T(8,128)(2,1)}) custom-call(bf16[256,1024]{1,0:T(8,128)(2,1)} %q_hbm.1, bf16[256,128]{1,0:T(8,128)(2,1)} %k_hbm.1, bf16[256,128]{1,0:T(8,128)(2,1)} %v_hbm.1, bf16[1024,8192]{1,0:T(8,128)(2,1)} %w_hbm.1, bf16[256,2048]{1,0:T(8,128)(2,1)} %x_hbm.1, bf16[256,2048]{1,0:T(8,128)(2,1)} %g_hbm.1, ...), custom_call_target="tpu_custom_call" | custom-call | flops 8999999488 | bytes 24000000 | tf_op jit(solution)/shard_map/pallas_call | solution.py:676
  54.7 2.2 %shard_map.123 = (bf16[256,1024]{1,0:T(8,128)(2,1)}, bf16[256,2048]{1,0:T(8,128)(2,1)}) custom-call(bf16[256,1024]{1,0:T(8,128)(2,1)} %get-tuple-element.4.a, bf16[256,2048]{1,0:T(8,128)(2,1)} %get-tuple-element.5.b), custom_call_target="tpu_custom_call" | custom-call | tf_op jit(solution)/shard_map/pallas_call | solution.py:695

commit v4 on v3

--- a/solution.py
+++ b/solution.py
@@ -456,25 +456,26 @@
         absorb(0, TOK, x - i, False)
         return 0
 
-    lax.fori_loop(1, x, earlier_row, 0)
-
-    @pl.when(x > 0)
-    def _():
-        wait_row(0)
-
-    @pl.when(x == SIDE - 1)
-    def _():
-        lax.fori_loop(1, RANKS, send_state, 0)
+    split = x // 2 + 1 - x // 2 * (1 - x // (SIDE - 1))
+    lax.fori_loop(1, split, earlier_row, 0)
 
     def last_row(half):
         @pl.when(x == 0)
         def _():
             absorb(half * HALF, HALF, 0, True)
 
-        @pl.when(x > 0)
-        def _():
-            absorb(half * HALF, HALF, 0, False)
-
+        def one_row(i, _):
+            if half == 0:
+                wait_row(x - i)
+
+                @pl.when((x == SIDE - 1) & (i == x))
+                def _():
+                    lax.fori_loop(1, RANKS, send_state, 0)
+
+            absorb(half * HALF, HALF, x - i, False)
+            return 0
+
+        lax.fori_loop(split, x + 1, one_row, 0)
         finish(half)
 
     last_row(0)

time: 58 us -> 57 us (0.983)
  Pallas kernels: 56.3 us -> 55.3 us
    pallas_call x1, Pallas kernels: 54.1 us -> 53.1 us  [local(): pl.pallas_call(kernel, out_shape=(jax.ShapeDtypeStruct((TOK, WIDE), BF16)...]
where the time goes in v4:
time: 57 us; the launch traced here: 56.1 us
  Pallas kernels  55.3 us (97%)
  between operations  0.8 us (1%)
    pallas_call x1, Pallas kernels, local(): pl.pallas_call(kernel, out_shape=(jax.ShapeDtypeStruct((TOK, WIDE), BF16)...  53.1 us
    pallas_call x1, Pallas kernels, local(): pl.pallas_call(place, out_shape=(jax.ShapeDtypeStruct((TOK, WIDE), BF16),...  2.24 us

profile of v4, /device:TPU:0, one launch (start us, length us, event | category | flops | bytes accessed | tf_op | source)
XLA Modules:
  0.0 56.1 jit_solution(8741100606139667142)
XLA Ops:
  0.6 53.1 %shard_map.122 = (bf16[256,1024]{1,0:T(8,128)(2,1)}, bf16[256,2048]{1,0:T(8,128)(2,1)}) custom-call(bf16[256,1024]{1,0:T(8,128)(2,1)} %q_hbm.1, bf16[256,128]{1,0:T(8,128)(2,1)} %k_hbm.1, bf16[256,128]{1,0:T(8,128)(2,1)} %v_hbm.1, bf16[1024,8192]{1,0:T(8,128)(2,1)} %w_hbm.1, bf16[256,2048]{1,0:T(8,128)(2,1)} %x_hbm.1, bf16[256,2048]{1,0:T(8,128)(2,1)} %g_hbm.1, ...), custom_call_target="tpu_custom_call" | custom-call | flops 8999999488 | bytes 24000000 | tf_op jit(solution)/shard_map/pallas_call | solution.py:677
  53.7 2.2 %shard_map.123 = (bf16[256,1024]{1,0:T(8,128)(2,1)}, bf16[256,2048]{1,0:T(8,128)(2,1)}) custom-call(bf16[256,1024]{1,0:T(8,128)(2,1)} %get-tuple-element.4.a, bf16[256,2048]{1,0:T(8,128)(2,1)} %get-tuple-element.5.b), custom_call_target="tpu_custom_call" | custom-call | tf_op jit(solution)/shard_map/pallas_call | solution.py:696
